TPU v7x, 32 devices: a whole 2x2x4 slice. The times are simulated.
32 devices in a mesh: ctx: 8 (over z, core), fsdp: 4 (over y, x).
Axes of the slice: x: 2, y: 2, z: 4, core: 2. Of those that a mesh axis runs over, the one named last changes fastest.
Arguments:
- tokens: bfloat16 [4, 1536, 2048], P('fsdp', 'ctx'), may hold values from -6 to 6
- cotangent: bfloat16 [4, 1536, 2048], P('fsdp', 'ctx'), may hold values from -6 to 6
- seq_lengths: int32 [4, 4], P('fsdp'), may hold values from 1 to 768, 1536 in all within a row
- token_order: int32 [4, 1536], P('fsdp'), may hold values from 0 to 1535, as said below
- ln_gain: bfloat16 [2048], P('fsdp'), may hold values from 0.5 to 1.5
- ln_bias: bfloat16 [2048], P('fsdp'), may hold values from -1.1953125 to 1.1953125
- w_qkv: bfloat16 [2048, 6144], P('fsdp'), may hold values from -0.125 to 0.125
- q_bias: bfloat16 [2048], P('fsdp'), may hold values from -3 to 3
- k_bias: bfloat16 [1024], P('fsdp'), may hold values from -3 to 3
- v_bias: bfloat16 [2048], P('fsdp'), may hold values from -3 to 3
- w_out: bfloat16 [2048, 2048], P('fsdp'), may hold values from -0.5 to 0.5
- out_bias: bfloat16 [2048], P('fsdp'), may hold values from -4 to 4
- w_up: bfloat16 [2048, 8192], P('fsdp'), may hold values from -0.125 to 0.125
- up_bias: bfloat16 [8192], P('fsdp'), may hold values from -1.1953125 to 1.1953125
- w_down: bfloat16 [8192, 2048], P('fsdp'), may hold values from -0.125 to 0.125
- down_bias: bfloat16 [2048], P('fsdp'), may hold values from -4 to 4
Outputs:
- out_act: bfloat16 [4, 1536, 2048], P('fsdp', 'ctx')
- d_tokens: float32 [4, 1536, 2048], P('fsdp', 'ctx')
- layernorm_gain_gradient: float32 [2048], P('fsdp')
- d_ln_bias: float32 [2048], P('fsdp')
- d_w_qkv: float32 [2048, 6144], P('fsdp')
- d_q_bias: float32 [2048], P('fsdp')
- d_k_bias: float32 [1024], P('fsdp')
- d_v_bias: float32 [2048], P('fsdp')
- d_w_out: float32 [2048, 2048], P('fsdp')
- d_out_bias: float32 [2048], P('fsdp')
- d_w_up: float32 [2048, 8192], P('fsdp')
- d_up_bias: float32 [8192], P('fsdp')
- d_w_down: float32 [8192, 2048], P('fsdp')
- d_down_bias: float32 [2048], P('fsdp')
Inputs may be any that keep to these rules, and one draw needn't show every extreme that they name: `seq_lengths`: lengths of a group's 4 sequences in the order in which they are laid end to end; each row sums to 1536. `token_order`: each row is a permutation; slots run device after device along ctx, 192 a device. Tokens r * (8) to (r + 1) * 8 - 1 lie on different devices.
All inputs are finite; a program needn't handle non-finite values.
Results may differ from a plain program's by a relative error of at most 0.035.
Values may be sent and summed in bfloat16 or wider, within the bound.
A program may use at most 576 MiB of HBM per device.

v0:
```python
import jax
import jax.numpy as jnp
from jax import lax
from jax.sharding import PartitionSpec as P

D = 2048
HEADS = 32
HD = 64
ROT = 32


def token_tables(length_row, order_row):
    bounds = jnp.cumsum(length_row)
    starts = bounds - length_row
    segment = jnp.sum((order_row[:, None] >= bounds[None, :]).astype(jnp.int32), axis=1)
    member = segment[:, None] == jnp.arange(length_row.shape[0], dtype=jnp.int32)[None, :]
    offset = jnp.sum(jnp.where(member, starts[None, :], 0), axis=1)
    return (segment, order_row - offset)


def rotary_tables(position):
    frequency = 10000.0 ** (-jnp.arange(ROT // 2, dtype=jnp.float32) * 2.0 / ROT)
    angles = position.astype(jnp.float32)[:, None] * frequency[None, :]
    return (jnp.cos(angles), jnp.sin(angles))


def rotate(values, cosine_table, sine_table):
    half = ROT // 2
    front_half = values[..., :half]
    back_half = values[..., half:ROT]
    remainder = values[..., ROT:]
    cosine_part = cosine_table[:, None, :]
    sine_part = sine_table[:, None, :]
    return jnp.concatenate(
        [
            front_half * cosine_part - back_half * sine_part,
            back_half * cosine_part + front_half * sine_part,
            remainder,
        ],
        axis=-1,
    )


def unrotate(grads, cosine_table, sine_table):
    half = ROT // 2
    front_half = grads[..., :half]
    back_half = grads[..., half:ROT]
    remainder = grads[..., ROT:]
    cosine_part = cosine_table[:, None, :]
    sine_part = sine_table[:, None, :]
    return jnp.concatenate(
        [
            front_half * cosine_part + back_half * sine_part,
            back_half * cosine_part - front_half * sine_part,
            remainder,
        ],
        axis=-1,
    )


def masked_scores(queries_low, key_block, own_order, own_segment, order_block, segment_block):
    allowed = (own_segment[:, None] == segment_block[None, :]) & (
        order_block[None, :] <= own_order[:, None]
    )
    scores = (
        jnp.einsum("qhd,khd->hqk", queries_low, key_block, preferred_element_type=jnp.float32)
        * 0.125
    )
    return (jnp.where(allowed[None], scores, -1e30), allowed)


def key_blocks(whole_keys, whole_values, order_row, segment):
    key_total = whole_keys.shape[0]
    block = 512
    blocks = key_total // block
    return (
        whole_keys.reshape(blocks, block, HEADS, HD),
        whole_values.reshape(blocks, block, HEADS, HD),
        order_row.reshape(blocks, block),
        segment.reshape(blocks, block),
    )


def attend_forward(queries_low, blocked, own_order, own_segment):
    local_rows = queries_low.shape[0]

    def total_step(carry, pieces):
        running, total = carry
        key_block, value_block, order_block, segment_block = pieces
        scores, allowed = masked_scores(
            queries_low, key_block, own_order, own_segment, order_block, segment_block
        )
        top_score = jnp.maximum(running, jnp.max(scores, axis=-1))
        weights = jnp.where(allowed[None], jnp.exp(scores - top_score[..., None]), 0.0)
        total = total * jnp.exp(running - top_score) + jnp.sum(weights, axis=-1)
        return ((top_score, total), None)

    start_carry = (
        jnp.full((HEADS, local_rows), -1e30, jnp.float32),
        jnp.zeros((HEADS, local_rows), jnp.float32),
    )
    (running, total), unused = lax.scan(total_step, start_carry, blocked)
    log_total = running + jnp.log(total)

    def mix_step(accum, pieces):
        key_block, value_block, order_block, segment_block = pieces
        scores, allowed = masked_scores(
            queries_low, key_block, own_order, own_segment, order_block, segment_block
        )
        probs_low = jnp.exp(scores - log_total[..., None]).astype(jnp.bfloat16)
        return (
            accum
            + jnp.einsum(
                "hqk,khd->qhd", probs_low, value_block, preferred_element_type=jnp.float32
            ),
            None,
        )

    mixed, unused = lax.scan(mix_step, jnp.zeros((local_rows, HEADS, HD), jnp.float32), blocked)
    return (mixed, log_total)


def attend_backward(queries_low, blocked, own_order, own_segment, log_total, d_attn_low, delta):
    local_rows = queries_low.shape[0]

    def back_step(dquery, pieces):
        key_block, value_block, order_block, segment_block = pieces
        scores, allowed = masked_scores(
            queries_low, key_block, own_order, own_segment, order_block, segment_block
        )
        probs = jnp.exp(scores - log_total[..., None])
        probs_low = probs.astype(jnp.bfloat16)
        dprobs = jnp.einsum(
            "qhd,khd->hqk", d_attn_low, value_block, preferred_element_type=jnp.float32
        )
        dscores_low = (probs * (dprobs - delta[..., None])).astype(jnp.bfloat16)
        dquery = dquery + 0.125 * jnp.einsum(
            "hqk,khd->qhd", dscores_low, key_block, preferred_element_type=jnp.float32
        )
        dkey = 0.125 * jnp.einsum(
            "hqk,qhd->khd", dscores_low, queries_low, preferred_element_type=jnp.float32
        )
        dvalue = jnp.einsum(
            "hqk,qhd->khd", probs_low, d_attn_low, preferred_element_type=jnp.float32
        )
        return (dquery, (dkey, dvalue))

    dquery, (dkey, dvalue) = lax.scan(
        back_step, jnp.zeros((local_rows, HEADS, HD), jnp.float32), blocked
    )
    key_total = dkey.shape[0] * dkey.shape[1]
    return (dquery, dkey.reshape(key_total, D), dvalue.reshape(key_total, D))


def body(
    tokens,
    cotangent,
    seq_lengths,
    token_order,
    ln_gain,
    ln_bias,
    w_qkv,
    q_bias,
    k_bias,
    v_bias,
    w_out,
    out_bias,
    w_up,
    up_bias,
    w_down,
    down_bias,
):
    attn_params = (
        lax.all_gather(ln_gain, "fsdp", axis=0, tiled=True),
        lax.all_gather(ln_bias, "fsdp", axis=0, tiled=True),
        lax.all_gather(w_qkv, "fsdp", axis=0, tiled=True),
        lax.all_gather(q_bias, "fsdp", axis=0, tiled=True),
        lax.all_gather(k_bias, "fsdp", axis=0, tiled=True),
        lax.all_gather(v_bias, "fsdp", axis=0, tiled=True),
        lax.all_gather(w_out, "fsdp", axis=0, tiled=True),
        lax.all_gather(out_bias, "fsdp", axis=0, tiled=True),
    )
    mlp_params = (
        lax.all_gather(w_up, "fsdp", axis=0, tiled=True),
        lax.all_gather(up_bias, "fsdp", axis=0, tiled=True),
        lax.all_gather(w_down, "fsdp", axis=0, tiled=True),
        lax.all_gather(down_bias, "fsdp", axis=0, tiled=True),
    )
    (
        gain_expanded,
        shift_bias_expanded,
        qkv_full,
        qbias_full,
        kbias_full,
        vbias_full,
        wout_full,
        obias_full,
    ) = attn_params
    wup_full, ubias_full, wdown_full, dbias_full = mlp_params
    local_rows = tokens.shape[1]
    order_row = token_order[0]
    segment, position = token_tables(seq_lengths[0], order_row)
    here = lax.axis_index("ctx") * local_rows
    own_order = lax.dynamic_slice_in_dim(order_row, here, local_rows)
    own_segment = lax.dynamic_slice_in_dim(segment, here, local_rows)
    own_position = lax.dynamic_slice_in_dim(position, here, local_rows)
    cosine_table, sine_table = rotary_tables(own_position)
    tokens_f = tokens[0].astype(jnp.float32)
    average = jnp.mean(tokens_f, axis=-1, keepdims=True)
    centered_input = tokens_f - average
    variance = jnp.mean(centered_input * centered_input, axis=-1, keepdims=True)
    inverse_deviation = lax.rsqrt(variance + 1e-05)
    standardized_input = centered_input * inverse_deviation
    normalized_reduced_precision = (
        standardized_input * gain_expanded.astype(jnp.float32)
        + shift_bias_expanded.astype(jnp.float32)
    ).astype(jnp.bfloat16)
    key_pad = jnp.pad(
        kbias_full.astype(jnp.float32).reshape(HEADS, ROT), ((0, 0), (0, HD - ROT))
    ).reshape(D)
    bias_all = jnp.concatenate(
        [qbias_full.astype(jnp.float32), key_pad, vbias_full.astype(jnp.float32)]
    )
    projected = (
        jnp.dot(normalized_reduced_precision, qkv_full, preferred_element_type=jnp.float32)
        + bias_all
    )
    queries_low = rotate(
        projected[:, :D].reshape(local_rows, HEADS, HD), cosine_table, sine_table
    ).astype(jnp.bfloat16)
    keys_low = (
        rotate(projected[:, D : 2 * D].reshape(local_rows, HEADS, HD), cosine_table, sine_table)
        .astype(jnp.bfloat16)
        .reshape(local_rows, D)
    )
    values_low = projected[:, 2 * D :].astype(jnp.bfloat16)
    whole_keys, whole_values = (
        lax.all_gather(keys_low, "ctx", axis=0, tiled=True),
        lax.all_gather(values_low, "ctx", axis=0, tiled=True),
    )
    blocked = key_blocks(whole_keys, whole_values, order_row, segment)
    mixed, log_total = attend_forward(queries_low, blocked, own_order, own_segment)
    attended_low = mixed.reshape(local_rows, D).astype(jnp.bfloat16)
    hidden = jnp.dot(
        normalized_reduced_precision, wup_full, preferred_element_type=jnp.float32
    ) + ubias_full.astype(jnp.float32)
    activated, gelu_back = jax.vjp(lambda inner: jax.nn.gelu(inner, approximate=True), hidden)
    activated_low = activated.astype(jnp.bfloat16)
    attn_branch = jnp.dot(
        attended_low, wout_full, preferred_element_type=jnp.float32
    ) + obias_full.astype(jnp.float32)
    mlp_branch = jnp.dot(
        activated_low, wdown_full, preferred_element_type=jnp.float32
    ) + dbias_full.astype(jnp.float32)
    out_act = (tokens_f + attn_branch + mlp_branch).astype(jnp.bfloat16)
    dy_low = cotangent[0]
    dy_f = dy_low.astype(jnp.float32)
    back_wup, back_wdown = (
        lax.all_gather(w_up, "fsdp", axis=0, tiled=True),
        lax.all_gather(w_down, "fsdp", axis=0, tiled=True),
    )
    piece = activated_low
    d_w_down = lax.psum_scatter(
        jnp.einsum("ti,tj->ij", piece, dy_low, preferred_element_type=jnp.float32).astype(
            jnp.bfloat16
        ),
        "fsdp",
        scatter_dimension=0,
        tiled=True,
    )
    d_act = jnp.einsum("tj,fj->tf", dy_low, back_wdown, preferred_element_type=jnp.float32)
    d_hidden_low = gelu_back(d_act)[0].astype(jnp.bfloat16)
    piece = normalized_reduced_precision
    d_w_up = lax.psum_scatter(
        jnp.einsum("ti,tf->if", piece, d_hidden_low, preferred_element_type=jnp.float32).astype(
            jnp.bfloat16
        ),
        "fsdp",
        scatter_dimension=0,
        tiled=True,
    )
    d_up_bias = jnp.sum(d_hidden_low.astype(jnp.float32), axis=0)
    d_normed_mlp = jnp.einsum(
        "tf,if->ti", d_hidden_low, back_wup, preferred_element_type=jnp.float32
    )
    d_out_bias = jnp.sum(dy_f, axis=0)
    d_down_bias = jnp.sum(dy_f, axis=0)
    back_gain_low, back_qkv, back_wout = (
        lax.all_gather(ln_gain, "fsdp", axis=0, tiled=True),
        lax.all_gather(w_qkv, "fsdp", axis=0, tiled=True),
        lax.all_gather(w_out, "fsdp", axis=0, tiled=True),
    )
    backward_gain_vector = back_gain_low.astype(jnp.float32)
    piece = attended_low
    d_w_out = lax.psum_scatter(
        jnp.einsum("ti,tj->ij", piece, dy_low, preferred_element_type=jnp.float32).astype(
            jnp.bfloat16
        ),
        "fsdp",
        scatter_dimension=0,
        tiled=True,
    )
    d_attn_low = (
        jnp.einsum("tj,ij->ti", dy_low, back_wout, preferred_element_type=jnp.float32)
        .astype(jnp.bfloat16)
        .reshape(local_rows, HEADS, HD)
    )
    delta = jnp.einsum("qhd,qhd->hq", d_attn_low.astype(jnp.float32), mixed)
    back_keys, back_values = (
        lax.all_gather(keys_low, "ctx", axis=0, tiled=True),
        lax.all_gather(values_low, "ctx", axis=0, tiled=True),
    )
    back_blocked = key_blocks(back_keys, back_values, order_row, segment)
    dquery, dkey_all, dvalue_all = attend_backward(
        queries_low, back_blocked, own_order, own_segment, log_total, d_attn_low, delta
    )
    dkey_own, dvalue_own = (
        lax.psum_scatter(
            dkey_all.astype(jnp.bfloat16), "ctx", scatter_dimension=0, tiled=True
        ).astype(jnp.float32),
        lax.psum_scatter(
            dvalue_all.astype(jnp.bfloat16), "ctx", scatter_dimension=0, tiled=True
        ).astype(jnp.float32),
    )
    dquery_pre = unrotate(dquery, cosine_table, sine_table).reshape(local_rows, D)
    dkey_pre = unrotate(dkey_own.reshape(local_rows, HEADS, HD), cosine_table, sine_table).reshape(
        local_rows, D
    )
    d_projected_low = jnp.concatenate([dquery_pre, dkey_pre, dvalue_own], axis=1).astype(
        jnp.bfloat16
    )
    piece = normalized_reduced_precision
    d_w_qkv = lax.psum_scatter(
        jnp.einsum("ti,tj->ij", piece, d_projected_low, preferred_element_type=jnp.float32).astype(
            jnp.bfloat16
        ),
        "fsdp",
        scatter_dimension=0,
        tiled=True,
    )
    column_sums = jnp.sum(d_projected_low.astype(jnp.float32), axis=0)
    d_q_bias = column_sums[:D]
    d_k_bias = column_sums[D : 2 * D].reshape(HEADS, HD)[:, :ROT].reshape(HEADS * ROT)
    d_v_bias = column_sums[2 * D :]
    normalized_gradient = (
        jnp.einsum("tj,ij->ti", d_projected_low, back_qkv, preferred_element_type=jnp.float32)
        + d_normed_mlp
    )
    layernorm_gain_gradient = jnp.sum(normalized_gradient * standardized_input, axis=0)
    d_ln_bias = jnp.sum(normalized_gradient, axis=0)
    standardized_gradient = normalized_gradient * backward_gain_vector
    d_inner = inverse_deviation * (
        standardized_gradient
        - jnp.mean(standardized_gradient, axis=-1, keepdims=True)
        - standardized_input
        * jnp.mean(standardized_gradient * standardized_input, axis=-1, keepdims=True)
    )
    d_tokens = dy_f + d_inner
    small = (
        lax.psum_scatter(
            layernorm_gain_gradient.astype(jnp.bfloat16), "fsdp", scatter_dimension=0, tiled=True
        ).astype(jnp.float32),
        lax.psum_scatter(
            d_ln_bias.astype(jnp.bfloat16), "fsdp", scatter_dimension=0, tiled=True
        ).astype(jnp.float32),
        lax.psum_scatter(
            d_q_bias.astype(jnp.bfloat16), "fsdp", scatter_dimension=0, tiled=True
        ).astype(jnp.float32),
        lax.psum_scatter(
            d_k_bias.astype(jnp.bfloat16), "fsdp", scatter_dimension=0, tiled=True
        ).astype(jnp.float32),
        lax.psum_scatter(
            d_v_bias.astype(jnp.bfloat16), "fsdp", scatter_dimension=0, tiled=True
        ).astype(jnp.float32),
        lax.psum_scatter(
            d_out_bias.astype(jnp.bfloat16), "fsdp", scatter_dimension=0, tiled=True
        ).astype(jnp.float32),
        lax.psum_scatter(
            d_up_bias.astype(jnp.bfloat16), "fsdp", scatter_dimension=0, tiled=True
        ).astype(jnp.float32),
        lax.psum_scatter(
            d_down_bias.astype(jnp.bfloat16), "fsdp", scatter_dimension=0, tiled=True
        ).astype(jnp.float32),
    )
    totals = (
        lax.psum(small[0].astype(jnp.bfloat16), "ctx").astype(jnp.float32),
        lax.psum(small[1].astype(jnp.bfloat16), "ctx").astype(jnp.float32),
        lax.psum(d_w_qkv, "ctx").astype(jnp.float32),
        lax.psum(small[2].astype(jnp.bfloat16), "ctx").astype(jnp.float32),
        lax.psum(small[3].astype(jnp.bfloat16), "ctx").astype(jnp.float32),
        lax.psum(small[4].astype(jnp.bfloat16), "ctx").astype(jnp.float32),
        lax.psum(d_w_out, "ctx").astype(jnp.float32),
        lax.psum(small[5].astype(jnp.bfloat16), "ctx").astype(jnp.float32),
        lax.psum(d_w_up, "ctx").astype(jnp.float32),
        lax.psum(small[6].astype(jnp.bfloat16), "ctx").astype(jnp.float32),
        lax.psum(d_w_down, "ctx").astype(jnp.float32),
        lax.psum(small[7].astype(jnp.bfloat16), "ctx").astype(jnp.float32),
    )
    return (
        out_act[None],
        d_tokens[None],
        totals[0],
        totals[1],
        totals[2],
        totals[3],
        totals[4],
        totals[5],
        totals[6],
        totals[7],
        totals[8],
        totals[9],
        totals[10],
        totals[11],
    )


def solution(mesh):
    in_specs = (
        P("fsdp", "ctx", None),
        P("fsdp", "ctx", None),
        P("fsdp", None),
        P("fsdp", None),
        P("fsdp"),
        P("fsdp"),
        P("fsdp", None),
        P("fsdp"),
        P("fsdp"),
        P("fsdp"),
        P("fsdp", None),
        P("fsdp"),
        P("fsdp", None),
        P("fsdp"),
        P("fsdp", None),
        P("fsdp"),
    )
    out_specs = (
        P("fsdp", "ctx", None),
        P("fsdp", "ctx", None),
        P("fsdp"),
        P("fsdp"),
        P("fsdp", None),
        P("fsdp"),
        P("fsdp"),
        P("fsdp"),
        P("fsdp", None),
        P("fsdp"),
        P("fsdp", None),
        P("fsdp"),
        P("fsdp", None),
        P("fsdp"),
    )
    return jax.shard_map(body, mesh=mesh, in_specs=in_specs, out_specs=out_specs, check_vma=False)
```

profile of v0, /device:TPU:0, one launch (start us, length us, event | category | flops | bytes accessed | tf_op | source)
XLA Modules:
  0.0 2804.6 jit_solution(16886006451100332694)
XLA Ops:
  9.1 9.5 all-gather.3
  18.8 8.0 all-gather.4
  34.0 8.1 all-gather.1
  42.1 7.1 all-gather
  50.3 190.2 %all-gather.14.cloned.1.call-done = bf16[2048,6144]{1,0:T(8,128)(2,1)} async-done(((bf16[512,6144]{1,0:T(8,128)(2,1)}), bf16[2048,6144]{1,0:T(8,128)(2,1)}) %all-gather.14.cloned.1.call-update) | async-done | bytes 25165840 | tf_op jit(solution)/shard_map/all_gather | solution.py:176
  240.6 10.9 convolution_add_fusion.1
  268.7 61.3 %all-gather.20.cloned.1.call-done = bf16[2048,2048]{1,0:T(8,128)(2,1)} async-done(((bf16[512,2048]{1,0:T(8,128)(2,1)}), bf16[2048,2048]{1,0:T(8,128)(2,1)}) %all-gather.20.cloned.1.call-update) | async-done | bytes 8388624 | tf_op jit(solution)/shard_map/all_gather | solution.py:180
  330.1 7.2 convolution_convert_fusion.4
  339.7 57.3 %all-gather.18.cloned.1.call-done = bf16[1536,2048]{1,0:T(8,128)(2,1)} async-done(((bf16[192,2048]{1,0:T(8,128)(2,1)}), bf16[1536,2048]{1,0:T(8,128)(2,1)}) %all-gather.18.cloned.1.call-update) | async-done | bytes 6291472 | tf_op jit(solution)/shard_map/all_gather | solution.py:238
  397.1 18.7 reshape.412
  415.7 14.1 copy.74
  429.8 24.2 while.39
  454.0 8.6 all-gather.16.cloned.1.call-done
  462.6 18.6 reshape.411
  481.2 14.0 copy.73
  495.2 26.2 while.40
  495.4 8.4 bitcast_add_fusion.4
  504.0 8.6 bitcast_add_fusion.4
  512.8 8.6 bitcast_add_fusion.4
  524.1 70.8 %while.41 = (s32[]{:T(128)}, f32[192,32,64]{0,2,1:T(8,128)}, bf16[3,512,32,64]{1,3,2,0:T(8,128)(2,1)}, bf16[3,512,32,64]{1,3,2,0:T(8,128)(2,1)}, bf16[3,512,32,6...) while((s32[]{:T(128)}, f32[192,32,64]{0,2,1:T(8,128)}, ...), condition=%wide.region_12.13_spmd.clone, body=%wide.region_11.12_spmd.clone.sunk | while | flops 2047246336 | bytes 90781472 | solution.py:148
  594.9 18.4 copy.97
  613.3 17.9 reshape.398
  631.3 18.5 copy.98
  649.8 17.9 reshape.400
  679.4 20.5 reduce-scatter.19.cloned.1.call-done
  706.0 64.8 %reduce-scatter.21.cloned.1.call-done = bf16[192,2048]{1,0:T(8,128)(2,1)} async-done(((bf16[1536,2048]{1,0:T(8,128)(2,1)}), bf16[192,2048]{1,0:T(8,128)(2,1)}) %reduce-scatter.21.cloned.1.call-update) | async-done | bytes 786448
  777.5 17.8 convolution_convert_fusion.2
  796.1 8.7 all_gather.60
  804.8 263.5 %all-gather.22.cloned.1.call-done = bf16[2048,8192]{1,0:T(8,128)(2,1)} async-done(((bf16[512,8192]{1,0:T(8,128)(2,1)}), bf16[2048,8192]{1,0:T(8,128)(2,1)}) %all-gather.22.cloned.1.call-update) | async-done | bytes 33554448 | tf_op jit(solution)/shard_map/all_gather | solution.py:184
  1068.3 19.3 convolution_add_fusion
  1087.7 18.4 convolution_convert_fusion.1
  1106.4 261.0 %all-gather.24.cloned.1.call-done = bf16[8192,2048]{1,0:T(8,128)(2,1)} async-done(((bf16[2048,2048]{1,0:T(8,128)(2,1)}), bf16[8192,2048]{1,0:T(8,128)(2,1)}) %all-gather.24.cloned.1.call-update) | async-done | bytes 33554448 | tf_op jit(solution)/shard_map/all_gather | solution.py:186
  1367.4 20.7 fusion.105
  1388.1 16.2 convolution_convert_fusion
  1404.4 53.2 %reduce-scatter.17.cloned.1.call-done = bf16[512,2048]{1,0:T(8,128)(2,1)} async-done(((bf16[2048,2048]{1,0:T(8,128)(2,1)}), bf16[512,2048]{1,0:T(8,128)(2,1)}) %reduce-scatter.17.cloned.1.call-update) | async-done | bytes 2097168 | tf_op jit(solution)/shard_map/reduce_scatter | solution.py:295
  1457.5 225.1 %reduce-scatter.15.cloned.1.call-done = bf16[512,6144]{1,0:T(8,128)(2,1)} async-done(((bf16[2048,6144]{1,0:T(8,128)(2,1)}), bf16[512,6144]{1,0:T(8,128)(2,1)}) %reduce-scatter.15.cloned.1.call-update) | async-done | bytes 6291472 | tf_op jit(solution)/shard_map/reduce_scatter | solution.py:333
  1682.7 291.8 %reduce-scatter.25.cloned.1.call-done = bf16[2048,2048]{1,0:T(8,128)(2,1)} async-done(((bf16[8192,2048]{1,0:T(8,128)(2,1)}), bf16[2048,2048]{1,0:T(8,128)(2,1)}) %reduce-scatter.25.cloned.1.call-update) | async-done | bytes 8388624
  1974.4 291.9 %reduce-scatter.23.cloned.1.call-done = bf16[512,8192]{1,0:T(8,128)(2,1)} async-done(((bf16[2048,8192]{1,0:T(8,128)(2,1)}), bf16[512,8192]{1,0:T(8,128)(2,1)}) %reduce-scatter.23.cloned.1.call-update) | async-done | bytes 8388624
  2269.5 7.9 all-gather.6
  2277.5 7.5 all-gather.5
  2291.4 21.3 fusion.70
  2315.6 14.8 fusion.98
  2330.3 20.1 fusion.86
  2350.5 15.9 all-reduce.12
  2366.8 16.0 all-reduce.10
  2389.6 373.2 %all-reduce.15.cloned.1.call-done = (bf16[512,6144]{1,0:T(8,128)(2,1)}, bf16[512,2048]{1,0:T(8,128)(2,1)}, bf16[512,8192]{1,0:T(8,128)(2,1)}, bf16[2048,2048]{1,0:T(8,128)(2,1)}) async-done(((bf16[512,6144]{1,0:T(8,128)(2,1)}, bf16[512,2048]{1,0:T(8,128)(2,1)}, bf16[512,8192]{1,0:T(8,128)(2,1)}, bf16[2048,2048]{1,0:T(8,128)(2,1)}), (bf16[512,6144]{1,0:T(8,128)(2,1)}, bf16[512,2048]{1,0:T(8,128)(2,1)}, ...) | async-done | bytes 25165840 | tf_op jit(solution)/shard_map/psum | solution.py:388
  2773.5 11.7 convert_element_type.208
  2785.2 11.7 convert_element_type.211
  (275 shorter events, 181.8 us)
Async XLA Ops:
  7.2 42.0 %copy-start.34 = (s32[1,1536]{1,0:T(1,128)S(1)}, s32[1,1536]{1,0:T(1,128)}, u32[]{:S(2)}) copy-start(s32[1,1536]{1,0:T(1,128)} %param.25) | copy-start | bytes 18436
  7.3 42.3 %copy-start.3 = (bf16[1,192,2048]{2,1,0:T(8,128)(2,1)S(1)}, bf16[1,192,2048]{2,1,0:T(8,128)(2,1)}, u32[]{:S(2)}) copy-start(bf16[1,192,2048]{2,1,0:T(8,128)(2,1)} %param.22) | copy-start | bytes 2359300
  7.3 233.3 %all-gather.14.cloned.1.call-start = ((), (), s32[]{:S(2)}) async-start(), calls=%async_computation.6 | async-start | bytes 31457280 | tf_op jit(solution)/shard_map/all_gather | solution.py:176
  8.0 322.1 %all-gather.20.cloned.1.call-start = ((), (), s32[]{:S(2)}) async-start(), calls=%async_computation.9 | async-start | bytes 10485760 | tf_op jit(solution)/shard_map/all_gather | solution.py:180
  8.7 388.3 %all-gather.18.cloned.1.call-start = ((), (), s32[]{:S(2)}) async-start(), calls=%async_computation.8 | async-start | bytes 7077888 | tf_op jit(solution)/shard_map/all_gather | solution.py:238
  42.1 209.4 %copy-start.22 = (f32[4,1,512]{2,1,0:T(1,128)}, f32[4,1,512]{2,1,0:T(1,128)S(1)}, u32[]{:S(2)}) copy-start(f32[4,1,512]{2,1,0:T(1,128)S(1)} %convert_element_type.213) | copy-start | bytes 24580
  49.3 202.3 %copy-start.20 = (f32[4,1,512]{2,1,0:T(1,128)}, f32[4,1,512]{2,1,0:T(1,128)S(1)}, u32[]{:S(2)}) copy-start(f32[4,1,512]{2,1,0:T(1,128)S(1)} %convert_element_type.212) | copy-start | bytes 24580
  49.8 201.7 %copy-start.24 = (f32[192]{0:T(256)}, f32[192]{0:T(256)S(1)}, u32[]{:S(2)}) copy-start(f32[192]{0:T(256)S(1)} %broadcast_multiply_fusion.2) | copy-start | bytes 2308
  50.2 201.4 %copy-start.26 = (f32[192]{0:T(256)}, f32[192]{0:T(256)S(1)}, u32[]{:S(2)}) copy-start(f32[192]{0:T(256)S(1)} %add_rsqrt_fusion) | copy-start | bytes 2308
  50.3 210.6 %copy-start.28 = (f32[192,16]{0,1:T(8,128)}, f32[192,16]{0,1:T(8,128)S(1)}, u32[]{:S(2)}) copy-start(f32[192,16]{0,1:T(8,128)S(1)} %get-tuple-element.538) | copy-start | bytes 36868
  50.3 210.6 %copy-start.30 = (f32[192,16]{0,1:T(8,128)}, f32[192,16]{0,1:T(8,128)S(1)}, u32[]{:S(2)}) copy-start(f32[192,16]{0,1:T(8,128)S(1)} %get-tuple-element.539) | copy-start | bytes 36868
  251.6 3.3 copy-start.18
  259.5 70.6 %copy-start.7 = (bf16[1,192,2048]{2,1,0:T(8,128)(2,1)S(1)}, bf16[1,192,2048]{2,1,0:T(8,128)(2,1)}, u32[]{:S(2)}) copy-start(bf16[1,192,2048]{2,1,0:T(8,128)(2,1)} %param.23) | copy-start | bytes 2359300
  265.8 196.8 %all-gather.16.cloned.1.call-start = ((), (), s32[]{:S(2)}) async-start(), calls=%async_computation.7 | async-start | bytes 7077888 | tf_op jit(solution)/shard_map/all_gather | solution.py:239
  268.3 431.6 %reduce-scatter.19.cloned.1.call-start = ((), (), s32[]{:S(2)}) async-start(), calls=%async_computation.14 | async-start | bytes 7077888
  495.2 26.2 copy-start.17
  535.6 5.8 copy-start
  545.2 2.7 copy-start.1
  545.2 2.7 copy-start.33
  559.2 5.8 copy-start
  582.7 5.8 copy-start
  592.2 2.7 copy-start.1
  592.2 2.7 copy-start.33
  631.2 139.6 %reduce-scatter.21.cloned.1.call-start = ((), (), s32[]{:S(2)}) async-start(), calls=%async_computation.15 | async-start | bytes 7077888
  667.7 400.6 %all-gather.22.cloned.1.call-start = ((), (), s32[]{:S(2)}) async-start(), calls=%async_computation.10 | async-start | bytes 41943040 | tf_op jit(solution)/shard_map/all_gather | solution.py:184
  668.5 2.7 copy-start.8
  668.5 698.9 %all-gather.24.cloned.1.call-start = ((), (), s32[]{:S(2)}) async-start(), calls=%async_computation.11 | async-start | bytes 41943040 | tf_op jit(solution)/shard_map/all_gather | solution.py:186
  669.2 788.3 %reduce-scatter.17.cloned.1.call-start = ((), (), s32[]{:S(2)}) async-start(), calls=%async_computation.13 | async-start | bytes 10485760 | tf_op jit(solution)/shard_map/reduce_scatter | solution.py:295
  676.9 96.1 %copy-start.29 = (f32[192,16]{0,1:T(8,128)S(1)}, f32[192,16]{0,1:T(8,128)}, u32[]{:S(2)}) copy-start(f32[192,16]{0,1:T(8,128)} %copy-done.28) | copy-start | bytes 36868
  677.0 96.1 %copy-start.31 = (f32[192,16]{0,1:T(8,128)S(1)}, f32[192,16]{0,1:T(8,128)}, u32[]{:S(2)}) copy-start(f32[192,16]{0,1:T(8,128)} %copy-done.30) | copy-start | bytes 36868
  677.0 1005.7 %reduce-scatter.15.cloned.1.call-start = ((), (), s32[]{:S(2)}) async-start(), calls=%async_computation.12 | async-start | bytes 31457280 | tf_op jit(solution)/shard_map/reduce_scatter | solution.py:333
  703.1 71.5 %copy-start.19 = (bf16[192,32,32]{0,2,1:T(8,128)(2,1)S(1)}, bf16[192,32,32]{0,2,1:T(8,128)(2,1)}, u32[]{:S(2)}) copy-start(bf16[192,32,32]{0,2,1:T(8,128)(2,1)} %slice.131) | copy-start | bytes 1179652
  703.1 74.4 %copy-start.4 = (bf16[1,192,2048]{2,1,0:T(8,128)(2,1)S(1)}, bf16[1,192,2048]{2,1,0:T(8,128)(2,1)}, u32[]{:S(2)}) copy-start(bf16[1,192,2048]{2,1,0:T(8,128)(2,1)} %param.22) | copy-start | bytes 2359300
  703.1 74.4 %copy-start.21 = (f32[4,1,512]{2,1,0:T(1,128)S(1)}, f32[4,1,512]{2,1,0:T(1,128)}, u32[]{:S(2)}) copy-start(f32[4,1,512]{2,1,0:T(1,128)} %copy-done.20) | copy-start | bytes 24580
  703.1 74.4 %copy-start.23 = (f32[4,1,512]{2,1,0:T(1,128)S(1)}, f32[4,1,512]{2,1,0:T(1,128)}, u32[]{:S(2)}) copy-start(f32[4,1,512]{2,1,0:T(1,128)} %copy-done.22) | copy-start | bytes 24580
  703.1 74.4 %copy-start.25 = (f32[192]{0:T(256)S(1)}, f32[192]{0:T(256)}, u32[]{:S(2)}) copy-start(f32[192]{0:T(256)} %copy-done.24) | copy-start | bytes 2308
  703.1 74.4 %copy-start.27 = (f32[192]{0:T(256)S(1)}, f32[192]{0:T(256)}, u32[]{:S(2)}) copy-start(f32[192]{0:T(256)} %copy-done.26) | copy-start | bytes 2308
  773.0 4.5 copy-start.10
  795.4 1179.0 %reduce-scatter.25.cloned.1.call-start = ((), (), s32[]{:S(2)}) async-start(), calls=%async_computation.17 | async-start | bytes 41943040
  804.8 282.9 %copy-start.9 = (bf16[1,192,2048]{2,1,0:T(8,128)(2,1)S(1)}, bf16[1,192,2048]{2,1,0:T(8,128)(2,1)}, u32[]{:S(2)}) copy-start(bf16[1,192,2048]{2,1,0:T(8,128)(2,1)} %param.23) | copy-start | bytes 2359300
  1106.1 1160.2 %reduce-scatter.23.cloned.1.call-start = ((), (), s32[]{:S(2)}) async-start(), calls=%async_computation.16 | async-start | bytes 41943040
  1404.3 1358.5 %all-reduce.15.cloned.1.call-start = ((), (), s32[]{:S(2)}) async-start(), calls=%async_computation.18 | async-start | bytes 50331648 | tf_op jit(solution)/shard_map/psum | solution.py:388
  2266.3 3.2 copy-start.41
  2266.3 3.2 copy-start.42
  2266.3 18.6 copy-start.6
  2291.4 21.3 copy-start.11
  2384.0 412.9 %copy-start.35 = (f32[512]{0:T(512)}, f32[512]{0:T(512)S(1)}, u32[]{:S(2)}) copy-start(f32[512]{0:T(512)S(1)} %convert_element_type.206) | copy-start | bytes 6148
  2762.8 4.3 copy-start.16
  (19 other events, 26.6 us)
Sparse Core Ops, SparseCore 0:
  10.0 230.5 all-gather.13
  242.4 87.5 all-gather.19
  332.3 64.7 all-gather.17
  399.1 63.3 all-gather.15
  631.4 68.4 reduce-scatter.18
  702.6 68.1 reduce-scatter.20
  772.6 295.6 all-gather.21
  1070.2 297.2 all-gather.23
  1371.1 86.4 reduce-scatter.16
  1460.8 221.8 reduce-scatter.14
  1685.7 288.6 reduce-scatter.24
  1977.6 288.6 reduce-scatter.22
  2269.2 493.5 all-reduce.14
where the time goes:
time: 2810 us; the launch traced here: 2800 us
  waiting for transfers between devices  2170 us (77%)
  matrix products  282 us (10%)
  local copies, waits for them, and re-layouts  170 us (6%)
  blocking collectives  95.8 us (3%)
  other arithmetic  72 us (3%)
    unnamed x17, waiting for transfers between devices  672 us
    psum x1, waiting for transfers between devices, body(): lax.psum(d_w_qkv, 'ctx').astype(jnp.float32)  373 us
    all_gather x1, waiting for transfers between devices, body(): lax.all_gather(w_up, 'fsdp', axis=0, tiled=True)  264 us
    all_gather x1, waiting for transfers between devices, body(): lax.all_gather(w_down, 'fsdp', axis=0, tiled=True)  261 us
    reduce_scatter x1, waiting for transfers between devices, body(): lax.psum_scatter(jnp.einsum('ti,tj->ij', piece, d_projected_low, preferre...  225 us
    all_gather x1, waiting for transfers between devices, body(): lax.all_gather(w_qkv, 'fsdp', axis=0, tiled=True)  190 us
    unnamed x110, local copies, waits for them, and re-layouts  114 us
    all_gather x1, waiting for transfers between devices, body(): lax.all_gather(w_out, 'fsdp', axis=0, tiled=True)  61.3 us
  transfers between devices with their start and end apart: 13, of which 13 were waited for; matrix products, arithmetic and copies ran while one was open for 11% of the time, Pallas kernels for 0%

commit v1 on v0

v1 whole, which is shorter than its diff:
```python
import functools

import jax
import jax.numpy as jnp
from jax import lax
from jax.experimental import pallas as pl
from jax.experimental.pallas import tpu as pltpu
from jax.sharding import PartitionSpec as P

D = 2048
HEADS = 32
HD = 64
ROT = 32
FF = 8192
LANES = 128
BF = jnp.bfloat16
F32 = jnp.float32


def dot_nn(a, b):
    return lax.dot_general(a, b, (((1,), (0,)), ((), ())), preferred_element_type=F32)


def dot_nt(a, b):
    return lax.dot_general(a, b, (((1,), (1,)), ((), ())), preferred_element_type=F32)


def dot_tn(a, b):
    return lax.dot_general(a, b, (((0,), (0,)), ((), ())), preferred_element_type=F32)


def wide(table, width):
    return jnp.concatenate([table] * (width // LANES), axis=1)


def partner(values):
    width = values.shape[1]
    lane = lax.broadcasted_iota(jnp.int32, values.shape, 1) % HD
    half = ROT // 2
    return jnp.where(
        lane < half, pltpu.roll(values, width - half, 1), pltpu.roll(values, half, 1)
    )


def sort_norm_project(
    x_ref, rank_ref, gain_ref, shift_ref, w_ref, bias_ref, cos_ref, sin_ref,
    normed_ref, q_ref, k_ref, v_ref,
):
    rows = x_ref.shape[1]
    width = q_ref.shape[2]
    place = lax.broadcasted_iota(jnp.int32, (rows, rows), 0)
    pick = jnp.where(rank_ref[0] == place, 1.0, 0.0).astype(BF)
    x = dot_nn(pick, x_ref[0])
    mean = jnp.mean(x, axis=1, keepdims=True)
    centered = x - mean
    variance = jnp.mean(centered * centered, axis=1, keepdims=True)
    normed = (centered * lax.rsqrt(variance + 1e-05) * gain_ref[...] + shift_ref[...]).astype(BF)
    normed_ref[0] = normed
    projected = dot_nn(normed, w_ref[...]) + bias_ref[...]
    cosine, sine = wide(cos_ref[0], width), wide(sin_ref[0], width)
    q = projected[:, :width]
    k = projected[:, width : 2 * width]
    q = (q * cosine + partner(q) * sine).astype(BF)
    q_ref[0] = (q.astype(F32) * 0.125).astype(BF)
    k_ref[0] = (k * cosine + partner(k) * sine).astype(BF)
    v_ref[0] = projected[:, 2 * width :].astype(BF)


def qkv_call(x_all, rank, gain, shift, weights, bias, cosine, sine):
    dealers, rows, _ = x_all.shape
    width = weights.shape[1] // 3
    whole = lambda *shape: pl.BlockSpec(shape, lambda i: (0,) * len(shape))
    each = lambda *shape: pl.BlockSpec((1,) + shape, lambda i: (i, 0, 0))
    out = lambda w: jax.ShapeDtypeStruct((dealers, rows, w), BF)
    return pl.pallas_call(
        sort_norm_project,
        name="sort_norm_project",
        grid=(dealers,),
        in_specs=[
            each(rows, D), each(1, rows), whole(1, D), whole(1, D),
            whole(D, 3 * width), whole(1, 3 * width), each(rows, LANES), each(rows, LANES),
        ],
        out_specs=[each(rows, D)] + [each(rows, width)] * 3,
        out_shape=[out(D), out(width), out(width), out(width)],
        compiler_params=pltpu.CompilerParams(vmem_limit_bytes=48 * 2**20),
    )(x_all, rank, gain, shift, weights, bias, cosine, sine)


def flash_forward(low_ref, q_ref, col_ref, row_ref, k_ref, v_ref, o_ref, of_ref, lse_ref):
    block = pl.program_id(0)
    dealers, rounds, width = q_ref.shape
    size = dealers * rounds
    heads = width // HD
    q = q_ref[...].reshape(size, width)
    col = col_ref[...].reshape(size, 2)
    top, bottom = col[:, 0:1], col[:, 1:2]
    head_of = lax.broadcasted_iota(jnp.int32, (size, width), 1) // HD
    q_of = [jnp.where(head_of == h, q, jnp.zeros_like(q)) for h in range(heads)]

    def step(j, carry):
        at = block - j
        running, total, mixed = carry
        window = pl.ds(pl.multiple_of(at * rounds, rounds), rounds)
        k = k_ref[:, window, :].reshape(size, width)
        v = v_ref[:, window, :].reshape(size, width)
        order = row_ref[at]
        allowed = (order <= top) & (order >= bottom)
        new_running, new_total = [], []
        for h in range(heads):
            scores = jnp.where(allowed, dot_nt(q_of[h], k), -1e30)
            peak = jnp.maximum(running[h], jnp.max(scores, axis=1, keepdims=True))
            probs = jnp.exp(scores - peak)
            scale = jnp.exp(running[h] - peak)
            new_running.append(peak)
            new_total.append(total[h] * scale + jnp.sum(probs, axis=1, keepdims=True))
            mixed = jnp.where(head_of == h, mixed * scale + dot_nn(probs.astype(BF), v), mixed)
        return (new_running, new_total, mixed)

    start = (
        [jnp.full((size, 1), -1e30, F32)] * heads,
        [jnp.zeros((size, 1), F32)] * heads,
        jnp.zeros((size, width), F32),
    )
    running, total, mixed = lax.fori_loop(0, block - low_ref[block] + 1, step, start)
    weight = jnp.zeros((size, width), F32)
    for h in range(heads):
        weight = jnp.where(head_of == h, 1.0 / total[h], weight)
    mixed = mixed * weight
    o_ref[...] = mixed.astype(BF).reshape(dealers, rounds, width)
    of_ref[...] = mixed.reshape(dealers, rounds, width)
    lse = [running[h] + jnp.log(total[h]) for h in range(heads)]
    lse_ref[...] = jnp.concatenate(lse, axis=1).reshape(dealers, rounds, heads)


def flash_forward_call(low, q, k, v, col, row):
    dealers, rows, width = q.shape
    rounds = 256 // dealers
    heads = width // HD
    part = lambda w: pl.BlockSpec((dealers, rounds, w), lambda i, low: (0, i, 0))
    whole = lambda shape: pl.BlockSpec(shape, lambda i, low: (0, 0, 0))
    return pl.pallas_call(
        flash_forward,
        name="flash_forward",
        grid_spec=pltpu.PrefetchScalarGridSpec(
            num_scalar_prefetch=1,
            grid=(rows // rounds,),
            in_specs=[part(width), part(2), whole(row.shape), whole(k.shape), whole(v.shape)],
            out_specs=[part(width), part(width), part(heads)],
        ),
        out_shape=[
            jax.ShapeDtypeStruct(q.shape, BF),
            jax.ShapeDtypeStruct(q.shape, F32),
            jax.ShapeDtypeStruct((dealers, rows, heads), F32),
        ],
        compiler_params=pltpu.CompilerParams(vmem_limit_bytes=48 * 2**20),
    )(low, q, col, row, k, v)


def flash_backward(
    low_ref, q_ref, da_ref, of_ref, lse_ref, col_ref, row_ref, k_ref, v_ref, cos_ref, sin_ref,
    d_ref, dk_acc, dv_acc,
):
    block = pl.program_id(0)
    dealers, rounds, width = q_ref.shape
    size = dealers * rounds
    heads = width // HD
    blocks = pl.num_programs(0)

    @pl.when(block == 0)
    def clear():
        dk_acc[...] = jnp.zeros_like(dk_acc)
        dv_acc[...] = jnp.zeros_like(dv_acc)

    q = q_ref[...].reshape(size, width)
    da = da_ref[...].reshape(size, width)
    col = col_ref[...].reshape(size, 2)
    lse = lse_ref[...].reshape(size, heads)
    top, bottom = col[:, 0:1], col[:, 1:2]
    head_of = lax.broadcasted_iota(jnp.int32, (size, width), 1) // HD
    product = da.astype(F32) * of_ref[...].reshape(size, width)
    q_of, da_of, delta = [], [], []
    for h in range(heads):
        q_of.append(jnp.where(head_of == h, q, jnp.zeros_like(q)))
        da_of.append(jnp.where(head_of == h, da, jnp.zeros_like(da)))
        delta.append(jnp.sum(jnp.where(head_of == h, product, 0.0), axis=1, keepdims=True))
    q_turned = q.astype(F32).T.astype(BF)
    da_turned = da.astype(F32).T.astype(BF)

    def step(at, dq):
        window = pl.ds(pl.multiple_of(at * rounds, rounds), rounds)
        k = k_ref[:, window, :].reshape(size, width)
        v = v_ref[:, window, :].reshape(size, width)
        order = row_ref[at]
        allowed = (order <= top) & (order >= bottom)
        for h in range(heads):
            scores = jnp.where(allowed, dot_nt(q_of[h], k), -1e30)
            probs = jnp.exp(scores - lse[:, h : h + 1])
            dprobs = dot_nt(da_of[h], v)
            dscores = (probs * (dprobs - delta[h])).astype(BF)
            own = slice(h * HD, (h + 1) * HD)
            dv_acc[at, own, :] += dot_nn(da_turned[own], probs.astype(BF))
            dk_acc[at, own, :] += dot_nn(q_turned[own], dscores)
            dq = jnp.where(head_of == h, dq + dot_nn(dscores, k), dq)
        return dq

    dq = lax.fori_loop(low_ref[block], block + 1, step, jnp.zeros((size, width), F32))

    def revert(grads, at):
        window = pl.ds(pl.multiple_of(at * rounds, rounds), rounds)
        cosine = wide(cos_ref[:, window, :].reshape(size, LANES), width)
        sine = wide(sin_ref[:, window, :].reshape(size, LANES), width)
        return grads * cosine - partner(grads) * sine

    def put(at, part, grads):
        window = pl.ds(pl.multiple_of(at * rounds, rounds), rounds)
        d_ref[:, window, part * width : (part + 1) * width] = grads.astype(BF).reshape(
            dealers, rounds, width
        )

    put(block, 0, revert(dq * 0.125, block))

    @pl.when(block == blocks - 1)
    def finish():
        def each(at, carry):
            put(at, 1, revert(dk_acc[at].T, at))
            put(at, 2, dv_acc[at].T)
            return carry

        lax.fori_loop(0, blocks, each, 0)


def flash_backward_call(low, q, da, of, lse, col, row, k, v, cosine, sine):
    dealers, rows, width = q.shape
    rounds = 256 // dealers
    heads = width // HD
    part = lambda w: pl.BlockSpec((dealers, rounds, w), lambda i, low: (0, i, 0))
    whole = lambda shape: pl.BlockSpec(shape, lambda i, low: (0, 0, 0))
    blocks = rows // rounds
    return pl.pallas_call(
        flash_backward,
        name="flash_backward",
        grid_spec=pltpu.PrefetchScalarGridSpec(
            num_scalar_prefetch=1,
            grid=(blocks,),
            in_specs=[
                part(width), part(width), part(width), part(heads), part(2), whole(row.shape),
                whole(k.shape), whole(v.shape), whole(cosine.shape), whole(sine.shape),
            ],
            out_specs=whole((dealers, rows, 3 * width)),
            scratch_shapes=[pltpu.VMEM((blocks, width, 256), F32)] * 2,
        ),
        out_shape=jax.ShapeDtypeStruct((dealers, rows, 3 * width), BF),
        compiler_params=pltpu.CompilerParams(vmem_limit_bytes=48 * 2**20),
    )(low, q, da, of, lse, col, row, k, v, cosine, sine)


def body(dealers, shards, *args):
    (
        tokens, cotangent, seq_lengths, token_order, ln_gain, ln_bias, w_qkv, q_bias, k_bias,
        v_bias, w_out, out_bias, w_up, up_bias, w_down, down_bias,
    ) = args
    rows = tokens.shape[1]
    count = dealers * rows
    me = lax.axis_index("ctx")
    shard = lax.axis_index("fsdp")
    width = D // dealers
    spread = HEADS % (dealers * shards) == 0
    head_piece = width // shards if spread else width
    unit_piece = FF // (dealers * shards)

    def over_ctx(value):
        return lax.all_gather(value, "ctx", axis=0, tiled=False)

    def over_fsdp(value):
        return lax.all_gather(value, "fsdp", axis=0, tiled=True)

    x_all = over_ctx(tokens[0])

    order_rows = token_order.reshape(dealers, rows)
    rank = order_rows // dealers
    places = jnp.arange(rows, dtype=jnp.int32)
    order = jnp.sum(
        jnp.where(rank[:, None, :] == places[None, :, None], order_rows[:, None, :], 0), axis=2
    )
    bounds = jnp.cumsum(seq_lengths[0])
    starts = bounds - seq_lengths[0]
    inside = (order[..., None] >= starts) & (order[..., None] < bounds)
    start = jnp.sum(jnp.where(inside, starts, 0), axis=-1)
    position = order - start
    frequency = 10000.0 ** (-jnp.arange(ROT // 2, dtype=F32) * 2.0 / ROT)
    zeros = jnp.zeros((HD - ROT,), F32)
    lane_frequency = jnp.tile(jnp.concatenate([frequency, frequency, zeros]), LANES // HD)
    sign = jnp.concatenate([-jnp.ones((ROT // 2,), F32), jnp.ones((ROT // 2,), F32), zeros])
    angles = position.astype(F32)[..., None] * lane_frequency
    cosine = jnp.cos(angles)
    sine = jnp.sin(angles) * jnp.tile(sign, LANES // HD)
    rounds = 256 // dealers
    blocks = rows // rounds
    row = order.reshape(dealers, blocks, rounds).transpose(1, 0, 2).reshape(blocks, 1, 256)
    col = jnp.stack([order, start], axis=-1)
    low = jnp.min(start.reshape(dealers, blocks, rounds), axis=(0, 2)) // 256

    own_rank = lax.dynamic_index_in_dim(rank, me, 0, keepdims=False)
    pick = (own_rank[None, :] == places[:, None]).astype(BF)
    dy_sorted = dot_nn(pick, cotangent[0]).astype(BF)
    dy_all = over_ctx(dy_sorted).reshape(count, D)

    small = jnp.concatenate(
        [ln_gain, ln_bias, q_bias, k_bias, v_bias, out_bias, up_bias, down_bias]
    )
    small = lax.all_gather(small, "fsdp", axis=0, tiled=False).astype(F32)
    vectors, at = [], 0
    for part in (ln_gain, ln_bias, q_bias, k_bias, v_bias, out_bias, up_bias, down_bias):
        vectors.append(small[:, at : at + part.shape[0]].reshape(shards * part.shape[0]))
        at += part.shape[0]
    gain, shift, qb, kb, vb, ob, ub, db = vectors
    kb = jnp.pad(kb.reshape(HEADS, ROT), ((0, 0), (0, HD - ROT))).reshape(D)

    def own_heads(matrix, axis):
        if not spread:
            return lax.dynamic_slice_in_dim(matrix, me * width, width, axis)
        return jnp.concatenate(
            [
                lax.dynamic_slice_in_dim(
                    matrix, j * (D // shards) + me * head_piece, head_piece, axis
                )
                for j in range(shards)
            ],
            axis=axis,
        )

    def own_units(matrix, axis):
        return jnp.concatenate(
            [
                lax.dynamic_slice_in_dim(
                    matrix, j * (FF // shards) + me * unit_piece, unit_piece, axis
                )
                for j in range(shards)
            ],
            axis=axis,
        )

    qkv_own = jnp.concatenate(
        [own_heads(w_qkv[:, i * D : (i + 1) * D], 1) for i in range(3)], axis=1
    )
    qkv_full = over_fsdp(qkv_own)
    bias_own = jnp.concatenate([own_heads(b, 0) for b in (qb, kb, vb)])
    up_full = over_fsdp(own_units(w_up, 1))
    up_bias_own = own_units(ub, 0)
    down_own = lax.dynamic_slice_in_dim(w_down, me * unit_piece, unit_piece, 0)
    if spread:
        out_own = lax.dynamic_slice_in_dim(w_out, me * head_piece, head_piece, 0)
        both = over_fsdp(jnp.concatenate([out_own, down_own], axis=0))
        both = both.reshape(shards, head_piece + unit_piece, D)
        out_full = both[:, :head_piece].reshape(width, D)
        down_full = both[:, head_piece:].reshape(FF // dealers, D)
    else:
        per = D // shards // width
        mine = lax.dynamic_slice_in_dim(w_out, (me % per) * width, width, 0)
        mine = jnp.where(me // per == shard, mine, jnp.zeros_like(mine))
        out_full = lax.psum(mine, "fsdp")
        down_full = over_fsdp(down_own)

    normed, q, k, v = qkv_call(
        x_all, rank[:, None, :], gain[None], shift[None], qkv_full, bias_own[None], cosine, sine
    )
    normed = normed.reshape(count, D)
    attn, attn_f, lse = flash_forward_call(low, q, k, v, col, row)
    attn = attn.reshape(count, width)
    hidden = dot_nn(normed, up_full) + up_bias_own[None]
    act, gelu_back = jax.vjp(lambda inner: jax.nn.gelu(inner, approximate=True), hidden)
    act = act.astype(BF)
    out_part = (dot_nn(attn, out_full) + dot_nn(act, down_full)).astype(BF)

    d_out = dot_tn(attn, dy_all).astype(BF)
    d_down = dot_tn(act, dy_all).astype(BF)
    scatter = functools.partial(lax.psum_scatter, scatter_dimension=0, tiled=True)
    if spread:
        d_both = jnp.concatenate(
            [d_out.reshape(shards, head_piece, D), d_down.reshape(shards, unit_piece, D)], axis=1
        )
        d_both = over_ctx(scatter(d_both.reshape(shards * (head_piece + unit_piece), D), "fsdp"))
        d_out = d_both[:, :head_piece].astype(F32).reshape(dealers * head_piece, D)
        d_down = d_both[:, head_piece:].astype(F32).reshape(dealers * unit_piece, D)
    else:
        d_out = lax.psum(d_out, "fsdp")
        d_out = jnp.where(me // per == shard, d_out, jnp.zeros_like(d_out))
        spot = jnp.zeros((per * width, D), BF)
        d_out = lax.dynamic_update_slice_in_dim(spot, d_out, (me % per) * width, 0)
        d_out = lax.psum(d_out, "ctx").astype(F32)
        d_down = over_ctx(scatter(d_down, "fsdp")).astype(F32).reshape(dealers * unit_piece, D)
    d_act = dot_nt(dy_all, down_full)
    d_hidden = gelu_back(d_act)[0].astype(BF)
    d_up = over_ctx(scatter(dot_tn(normed, d_hidden).astype(BF), "fsdp"))
    d_up = d_up.reshape(dealers, D // shards, shards, unit_piece).transpose(1, 2, 0, 3)
    d_up = d_up.astype(F32).reshape(D // shards, FF)

    d_attn = dot_nt(dy_all, out_full).astype(BF).reshape(dealers, rows, width)
    d_qkv = flash_backward_call(low, q, d_attn, attn_f, lse, col, row, k, v, cosine, sine)
    d_qkv = d_qkv.reshape(count, 3 * width)
    d_normed = (dot_nt(d_qkv, qkv_full) + dot_nt(d_hidden, up_full)).astype(BF)
    d_w_qkv = over_ctx(scatter(dot_tn(normed, d_qkv).astype(BF), "fsdp"))
    if spread:
        d_w_qkv = d_w_qkv.reshape(dealers, D // shards, 3, shards, head_piece)
        d_w_qkv = d_w_qkv.transpose(1, 2, 3, 0, 4)
    else:
        d_w_qkv = d_w_qkv.reshape(dealers, D // shards, 3, width).transpose(1, 2, 0, 3)
    d_w_qkv = d_w_qkv.astype(F32).reshape(D // shards, 3 * D)

    out_own = dot_tn(pick, scatter(out_part, "ctx"))
    x = tokens[0].astype(F32)
    out_act = (x + out_own + (ob + db)[None]).astype(BF)
    dn = dot_tn(pick, scatter(d_normed, "ctx"))
    mean = jnp.mean(x, axis=-1, keepdims=True)
    centered = x - mean
    variance = jnp.mean(centered * centered, axis=-1, keepdims=True)
    inverse = lax.rsqrt(variance + 1e-05)
    standard = centered * inverse
    grad = dn * gain[None]
    d_tokens = cotangent[0].astype(F32) + inverse * (
        grad
        - jnp.mean(grad, axis=-1, keepdims=True)
        - standard * jnp.mean(grad * standard, axis=-1, keepdims=True)
    )

    def place(vector, pieces):
        piece = vector.shape[0] // pieces
        mine = (jnp.arange(dealers) == me)[None, :, None]
        vector = vector.reshape(pieces, 1, piece)
        return jnp.where(mine, vector, 0.0).reshape(pieces * dealers * piece)

    head_pieces = shards if spread else 1
    sums = jnp.concatenate(
        [
            jnp.sum(dn * standard, axis=0),
            jnp.sum(dn, axis=0),
            jnp.sum(cotangent[0].astype(F32), axis=0),
            place(jnp.sum(d_qkv.astype(F32), axis=0), 3 * head_pieces),
            place(jnp.sum(d_hidden.astype(F32), axis=0), shards),
        ]
    )
    sums = lax.psum(sums, ("ctx", "fsdp"))

    def mine(vector):
        piece = vector.shape[0] // shards
        return lax.dynamic_slice_in_dim(vector, shard * piece, piece, 0)

    gain_sum, shift_sum, dy_sum, qkv_sum, up_sum = (
        sums[:D], sums[D : 2 * D], sums[2 * D : 3 * D], sums[3 * D : 6 * D], sums[6 * D :],
    )
    k_sum = qkv_sum[D : 2 * D].reshape(HEADS, HD)[:, :ROT].reshape(HEADS * ROT)
    return (
        out_act[None], d_tokens[None], mine(gain_sum), mine(shift_sum),
        d_w_qkv, mine(qkv_sum[:D]), mine(k_sum), mine(qkv_sum[2 * D :]),
        d_out, mine(dy_sum), d_up, mine(up_sum), d_down, mine(dy_sum),
    )


def solution(mesh):
    row, vector = P("fsdp", None), P("fsdp")
    split = P("fsdp", "ctx", None)
    in_specs = (
        split, split, row, row, vector, vector, row, vector,
        vector, vector, row, vector, row, vector, row, vector,
    )
    out_specs = (
        split, split, vector, vector, row, vector, vector, vector,
        row, vector, row, vector, row, vector,
    )
    step = functools.partial(body, mesh.shape["ctx"], mesh.shape["fsdp"])
    return jax.shard_map(
        step, mesh=mesh, in_specs=in_specs, out_specs=out_specs, check_vma=False
    )
```

time: 2810 us -> 1070 us (0.38)
  waiting for transfers between devices: 2170 us -> 681 us
  matrix products: 282 us -> 112 us
  blocking collectives: 95.8 us -> 10.5 us
  Pallas kernels: 0 us -> 59.7 us
  other arithmetic: 72 us -> 27.6 us
    unnamed x17 -> x14, waiting for transfers between devices: 672 us -> 0.89 us
    all_gather x6 -> x8, waiting for transfers between devices: 842 us -> 314 us  [the longest x5 227 us: over_ctx(): return lax.all_gather(value, 'ctx', axis=0, tiled=False)]
    psum x1, waiting for transfers between devices: 373 us -> 122 us  [body(): sums = lax.psum(sums, ('ctx', 'fsdp'))]
    dot_general x33 -> x14, matrix products: 282 us -> 112 us  [the longest x4 43.6 us: dot_nt(): lax.dot_general(a, b, (((1,), (1,)), ((), ())), preferred_element_type=F32)]
    pallas_call x0 -> x3, Pallas kernels: none -> 59.7 us  [the longest x1 25.4 us: flash_backward_call(): pl.pallas_call(flash_backward, name='flash_backward', grid_spec=pltpu.Pre...]
    all_gather x8 -> x1, blocking collectives: 63.9 us -> 10.5 us  [body(): small = lax.all_gather(small, 'fsdp', axis=0, tiled=False).astype(F32)]
    unnamed x110 -> x86, local copies, waits for them, and re-layouts: 114 us -> 60.3 us
    convert_element_type x18 -> x0, other arithmetic: 37.8 us -> none  [the longest x1 11.7 us: body(): lax.psum(d_w_up, 'ctx').astype(jnp.float32)]
  transfers between devices with their start and end apart: 13 -> 14, of which waited for: 13 -> 14; matrix products, arithmetic and copies ran while one was open for 11% -> 21% of each run, Pallas kernels for 0% -> 6%
where the time goes in v1:
time: 1070 us; the launch traced here: 1060 us
  waiting for transfers between devices  681 us (64%)
  local copies, waits for them, and re-layouts  156 us (15%)
  matrix products  112 us (10%)
  Pallas kernels  59.7 us (6%)
  other arithmetic  27.6 us (3%)
  between operations  14.9 us (1%)
    all_gather x5, waiting for transfers between devices, over_ctx(): return lax.all_gather(value, 'ctx', axis=0, tiled=False)  227 us
    psum x1, waiting for transfers between devices, body(): sums = lax.psum(sums, ('ctx', 'fsdp'))  122 us
    all_gather x3, waiting for transfers between devices, over_fsdp(): return lax.all_gather(value, 'fsdp', axis=0, tiled=True)  87 us
    reduce_scatter x1, waiting for transfers between devices, body(): out_own = dot_tn(pick, scatter(out_part, 'ctx'))  72.6 us
    reduce_scatter x1, waiting for transfers between devices, body(): scatter(d_both.reshape(shards * (head_piece + unit_piece), D), 'fsdp')  65.2 us
    unnamed x86, local copies, waits for them, and re-layouts  60.3 us
    reduce_scatter x1, waiting for transfers between devices, body(): d_up = over_ctx(scatter(dot_tn(normed, d_hidden).astype(BF), 'fsdp'))  55.6 us
    dot_general x4, matrix products, dot_nt(): lax.dot_general(a, b, (((1,), (1,)), ((), ())), preferred_element_type=F32)  43.6 us
  transfers between devices with their start and end apart: 14, of which 14 were waited for; matrix products, arithmetic and copies ran while one was open for 21% of the time, Pallas kernels for 6%

profile of v1, /device:TPU:0, one launch (start us, length us, event | category | flops | bytes accessed | tf_op | source)
XLA Modules:
  0.0 1062.7 jit_solution(6706236931816424121)
XLA Ops:
  10.3 4.0 fusion.34
  15.1 3.4 concatenate.28
  25.3 10.5 all-gather.5
  38.2 2.8 fusion.23
  41.0 34.3 %all-gather.19.cloned.1.call-done = bf16[1280,2048]{1,0:T(8,128)(2,1)} async-done(((bf16[320,2048]{1,0:T(8,128)(2,1)}), bf16[1280,2048]{1,0:T(8,128)(2,1)}) %all-gather.19.cloned.1.call-update) | async-done | bytes 5242896 | tf_op jit(solution)/shard_map/all_gather | solution.py:275
  75.3 4.8 slice.111
  80.1 2.4 slice.109
  82.4 39.3 %all-gather.17.cloned.1.call-done.w_ref = bf16[2048,768]{1,0:T(8,128)(2,1)} async-done(((bf16[512,768]{1,0:T(8,128)(2,1)}), bf16[2048,768]{1,0:T(8,128)(2,1)}) %all-gather.17.cloned.1.call-update) | async-done | bytes 3145744 | tf_op jit(solution)/shard_map/all_gather | solution.py:275
  121.7 66.4 %all-gather.15.cloned.1.call-done.x_ref = bf16[8,192,2048]{2,1,0:T(8,128)(2,1)} async-done(((bf16[1,192,2048]{2,1,0:T(8,128)(2,1)}), bf16[8,192,2048]{2,1,0:T(8,128)(2,1)}) %all-gather.15.cloned.1.call-update) | async-done | bytes 6291472 | tf_op jit(solution)/shard_map/all_gather | solution.py:272
  188.1 17.2 %sort_norm_project.1 = (bf16[8,192,2048]{2,1,0:T(8,128)(2,1)}, bf16[8,192,256]{2,1,0:T(8,128)(2,1)S(1)}, bf16[8,192,256]{2,1,0:T(8,128)(2,1)S(1)}, bf16[8,192,256]{2,1,0:T(8,128)(2,1)S(1)}) custom-call(bf16[8,192,2048]{2,1,0:T(8,128)(2,1)} %all-gather.15.cloned.1.call-done.x_ref, s32[8,1,192]{2,1,0:T(1,128)S(1)} %and_select_fusion.rank_ref, ...), custom_call_target="tpu_custom_call" | custom-call | tf_op jit(solution)/shard_map/sort_norm_project/pallas_call | solution.py:75
  205.3 17.1 %flash_forward.1 = (bf16[8,192,256]{2,1,0:T(8,128)(2,1)S(1)}, f32[8,192,256]{2,1,0:T(8,128)}, f32[8,192,4]{2,1,0:T(8,128)S(1)}) custom-call(s32[6]{0:T(128)S(1)} %and_select_fusion.1.low_ref, bf16[8,192,256]{2,1,0:T(8,128)(2,1)S(1)} %get-tuple-element.21.q_ref, s32[8,192,2]{2,1,0:T(8,128)S(1)} %copy.55.col_ref, s32[6,1,256]{2,1,0:T(1,128)S(1)} %reshape.304.row_ref, ...), custom_call_target="tpu_custom_call" | custom-call | tf_op jit(solution)/shard_map/flash_forward/pallas_call | solution.py:141
  225.2 28.5 %all-gather.23.cloned.1.call-done = bf16[1536,2048]{1,0:T(8,128)(2,1)} async-done(((bf16[192,2048]{1,0:T(8,128)(2,1)}), bf16[1536,2048]{1,0:T(8,128)(2,1)}) %all-gather.23.cloned.1.call-update) | async-done | bytes 6291472 | tf_op jit(solution)/shard_map/all_gather | solution.py:272
  253.7 5.0 convolution_convert_fusion.2
  258.7 25.4 %flash_backward.1 = bf16[8,192,768]{2,1,0:T(8,128)(2,1)} custom-call(s32[6]{0:T(128)S(1)} %and_select_fusion.1.low_ref, bf16[8,192,256]{2,1,0:T(8,128)(2,1)S(1)} %get-tuple-element.21.q_ref, bf16[8,192,256]{2,1,0:T(8,128)(2,1)S(1)} %bitcast.137, f32[8,192,256]{2,1,0:T(8,128)} %get-tuple-element.26.of_ref, f32[8,192,4]{2,1,0:T(8,128)S(1)} %copy-done.8, ...), custom_call_target="tpu_custom_call" | custom-call | tf_op jit(solution)/shard_map/flash_backward/pallas_call | solution.py:239
  284.1 9.7 fusion.42
  293.8 13.5 %all-gather.21.cloned.1.call-done = bf16[2048,1024]{1,0:T(8,128)(2,1)} async-done(((bf16[512,1024]{1,0:T(8,128)(2,1)}), bf16[2048,1024]{1,0:T(8,128)(2,1)}) %all-gather.21.cloned.1.call-update) | async-done | bytes 4194320 | tf_op jit(solution)/shard_map/all_gather | solution.py:275
  307.3 10.1 fusion.41
  317.5 16.5 %convert_reduce_fusion = (f32[1024]{0:T(1024)S(1)}, bf16[1536,1024]{1,0:T(8,128)(2,1)}) fusion(f32[1536,1024]{1,0:T(8,128)S(1)} %fusion.41, f32[1024]{0:T(1024)S(1)} %pad_maximum_fusion.3, bf16[1536,2048]{1,0:T(8,128)(2,1)} %all-gather.23.cloned.1.call-done, bf16[1024,2048]{1,0:T(8,128)(2,1)S(1)} %bitcast.157), kind=kOutput, calls=%fused_computation.13 | convolution fusion | flops 6478625792 | bytes 19931136 | tf_op jit(solution)/shard_map/dot_general | solution.py:25
  334.0 12.4 %add_convert_fusion = bf16[1536,2048]{1,0:T(8,128)(2,1)} fusion(f32[1536,2048]{1,0:T(8,128)} %fusion.42, bf16[1536,1024]{1,0:T(8,128)(2,1)} %get-tuple-element.89, bf16[2048,1024]{1,0:T(8,128)(2,1)S(1)} %copy-done.26), kind=kOutput, calls=%fused_computation | convolution fusion | flops 6448742400 | bytes 26214400 | tf_op jit(solution)/shard_map/dot_general | solution.py:25
  346.5 9.2 bitcast_convert_fusion.1
  355.7 11.4 %convolution_convert_fusion = bf16[2048,1024]{1,0:T(8,128)(2,1)} fusion(bf16[1536,2048]{1,0:T(8,128)(2,1)} %bitcast.178, bf16[1536,1024]{1,0:T(8,128)(2,1)} %get-tuple-element.89), kind=kOutput, calls=%fused_computation.17 | convolution fusion | flops 6444548096 | bytes 13631488 | tf_op jit(solution)/shard_map/dot_general | solution.py:29
  367.2 4.7 fusion.7
  371.8 11.9 %convolution_convert_fusion.1 = bf16[1024,2048]{1,0:T(8,128)(2,1)S(1)} fusion(bf16[1536,2048]{1,0:T(8,128)(2,1)} %all-gather.23.cloned.1.call-done, f32[1536,1024]{1,0:T(8,128)} %copy-done.29, f32[1024]{0:T(1024)S(1)} %pad_maximum_fusion.3), kind=kOutput, calls=%fused_computation.18 | convolution fusion | flops 6460276736 | bytes 16781312 | tf_op jit(solution)/shard_map/dot_general | solution.py:29
  383.7 2.8 pad_maximum_fusion
  386.6 11.2 %fusion.32 = f32[1536,2048]{1,0:T(8,128)S(1)} fusion(bf16[1024,2048]{1,0:T(8,128)(2,1)} %bitcast.156, f32[1536,1024]{1,0:T(8,128)} %copy-done.29, f32[1024]{0:T(1024)S(1)} %pad_maximum_fusion.3), kind=kOutput, calls=%fused_computation.120 | convolution fusion | flops 6458179584 | bytes 23072768 | tf_op jit(solution)/shard_map/dot_general | solution.py:21
  397.8 4.7 add_convert_fusion.1
  405.2 11.2 %reduce-scatter.8.cloned.1.call-done = bf16[192,2048]{1,0:T(8,128)(2,1)} async-done(((bf16[1536,2048]{1,0:T(8,128)(2,1)}), bf16[192,2048]{1,0:T(8,128)(2,1)}) %reduce-scatter.8.cloned.1.call-update) | async-done | bytes 786448 | tf_op jit(solution)/shard_map/reduce_scatter | solution.py:413
  416.4 2.0 fusion.20
  418.5 3.1 convert_reduce_fusion.2
  422.3 39.4 %reduce-scatter.10.cloned.1.call-done = bf16[512,768]{1,0:T(8,128)(2,1)} async-done(((bf16[2048,768]{1,0:T(8,128)(2,1)}), bf16[512,768]{1,0:T(8,128)(2,1)}) %reduce-scatter.10.cloned.1.call-update) | async-done | bytes 786448 | tf_op jit(solution)/shard_map/reduce_scatter | solution.py:402
  461.8 55.6 %reduce-scatter.14.cloned.1.call-done = bf16[512,1024]{1,0:T(8,128)(2,1)} async-done(((bf16[2048,1024]{1,0:T(8,128)(2,1)}), bf16[512,1024]{1,0:T(8,128)(2,1)}) %reduce-scatter.14.cloned.1.call-update) | async-done | bytes 1048592 | tf_op jit(solution)/shard_map/reduce_scatter | solution.py:394
  517.5 65.2 %reduce-scatter.12.cloned.1.call-done = bf16[320,2048]{1,0:T(8,128)(2,1)} async-done(((bf16[1280,2048]{1,0:T(8,128)(2,1)}), bf16[320,2048]{1,0:T(8,128)(2,1)}) %reduce-scatter.12.cloned.1.call-update) | async-done | bytes 1310736 | tf_op jit(solution)/shard_map/reduce_scatter | solution.py:382
  582.7 72.6 %reduce-scatter.6.cloned.1.call-done = bf16[192,2048]{1,0:T(8,128)(2,1)} async-done(((bf16[1536,2048]{1,0:T(8,128)(2,1)}), bf16[192,2048]{1,0:T(8,128)(2,1)}) %reduce-scatter.6.cloned.1.call-update) | async-done | bytes 786448 | tf_op jit(solution)/shard_map/reduce_scatter | solution.py:410
  655.4 2.4 fusion.10
  657.8 122.5 %all-reduce.3.cloned.1.call-done = f32[20480]{0:T(1024)} async-done(((f32[20480]{0:T(1024)}), f32[20480]{0:T(1024)}) %all-reduce.3.cloned.1.call-update) | async-done | bytes 81936 | tf_op jit(solution)/shard_map/psum | solution.py:442
  785.9 62.7 %all-gather.25.cloned.1.call-done = bf16[4096,768]{1,0:T(8,128)(2,1)} async-done(((bf16[512,768]{1,0:T(8,128)(2,1)}), bf16[4096,768]{1,0:T(8,128)(2,1)}) %all-gather.25.cloned.1.call-update) | async-done | bytes 6291472 | tf_op jit(solution)/shard_map/all_gather | solution.py:272
  848.6 9.7 copy.57
  858.3 22.2 %copy.70 = f32[96,8,8,512]{3,2,1,0:T(8,128)} copy(f32[96,8,8,512]{3,1,2,0:T(8,128)} %bitcast.142) | data formatting | bytes 25165824
  880.5 18.1 %copy.58 = f32[512,3,4,8,64]{0,4,3,2,1:T(8,128)} copy(f32[512,3,4,8,64]{0,3,4,2,1:T(8,128)} %bitcast.143) | data formatting | bytes 25165824 | tf_op jit(solution)/shard_map/reshape | solution.py:408
  898.6 12.6 %copy.60 = f32[512,6144]{1,0:T(8,128)} copy(f32[512,6144]{0,1:T(8,128)} %bitcast.144) | data formatting | bytes 25165824
  911.2 19.8 %all-gather.29.cloned.1.call-done = bf16[4096,1024]{1,0:T(8,128)(2,1)} async-done(((bf16[512,1024]{1,0:T(8,128)(2,1)}), bf16[4096,1024]{1,0:T(8,128)(2,1)}) %all-gather.29.cloned.1.call-update) | async-done | bytes 8388624 | tf_op jit(solution)/shard_map/all_gather | solution.py:272
  931.0 16.8 %reshape.340 = f32[8,512,4,256]{3,2,1,0:T(4,128)} reshape(bf16[4096,1024]{1,0:T(8,128)(2,1)} %all-gather.29.cloned.1.call-done) | data formatting | bytes 25165824 | tf_op jit(solution)/shard_map/reshape | solution.py:396
  947.9 15.5 %copy.59 = f32[512,4,8,256]{3,2,1,0:T(8,128)S(1)} copy(f32[512,4,8,256]{3,1,0,2:T(4,128)} %bitcast.140) | data formatting | bytes 33554432 | tf_op jit(solution)/shard_map/reshape | solution.py:396
  963.4 18.0 %copy.71 = f32[64,8,32,256]{3,1,2,0:T(8,128)} copy(f32[64,8,32,256]{3,2,1,0:T(8,128)S(1)} %bitcast.141) | data formatting | bytes 33554432
  981.4 49.2 %all-gather.27.cloned.1.call-done = bf16[2560,2048]{1,0:T(8,128)(2,1)} async-done(((bf16[320,2048]{1,0:T(8,128)(2,1)}), bf16[2560,2048]{1,0:T(8,128)(2,1)}) %all-gather.27.cloned.1.call-update) | async-done | bytes 10485776 | tf_op jit(solution)/shard_map/all_gather | solution.py:272
  1032.3 8.4 slice.123
  1040.7 2.7 bitcast_convert_fusion.2
  1043.4 11.8 %bitcast_convert_fusion = f32[2048,2048]{1,0:T(8,128)} fusion(bf16[8,256,2048]{2,1,0:T(8,128)(2,1)} %slice.123), kind=kLoop, calls=%fused_computation.4 | loop fusion | flops 4194304 | bytes 25165824 | tf_op jit(solution)/shard_map/reshape | solution.py:384
  (184 shorter events, 27.2 us)
Async XLA Ops:
  7.2 1.9 copy-start
  7.2 68.1 %all-gather.19.cloned.1.call-start = ((), (), s32[]{:S(2)}) async-start(), calls=%async_computation.7 | async-start | bytes 6553600 | tf_op jit(solution)/shard_map/all_gather | solution.py:275
  10.3 111.4 %all-gather.17.cloned.1.call-start = ((), (), s32[]{:S(2)}) async-start(), calls=%async_computation.6 | async-start | bytes 3932160 | tf_op jit(solution)/shard_map/all_gather | solution.py:275
  14.3 5.0 copy-start.17
  14.3 5.1 copy-start.14
  15.0 8.5 copy-start.19
  15.0 8.7 copy-start.20
  15.0 8.9 copy-start.21
  15.0 9.1 copy-start.25
  15.1 9.3 copy-start.22
  15.1 9.5 copy-start.23
  15.1 9.7 copy-start.18
  15.1 10.0 copy-start.24
  15.1 21.3 %copy-start.28 = (f32[64]{0:T(128)S(1)}, f32[64]{0:T(128)}, u32[]{:S(2)}) copy-start(f32[64]{0:T(128)} %constant.94.clone.1) | copy-start | bytes 772
  15.1 21.5 %copy-start.27 = (s32[1,4]{1,0:T(1,128)S(1)}, s32[1,4]{1,0:T(1,128)}, u32[]{:S(2)}) copy-start(s32[1,4]{1,0:T(1,128)} %param.18) | copy-start | bytes 52
  18.5 169.6 %all-gather.15.cloned.1.call-start = ((), (), s32[]{:S(2)}) async-start(), calls=%async_computation.5 | async-start | bytes 7077888 | tf_op jit(solution)/shard_map/all_gather | solution.py:272
  19.3 234.4 %all-gather.23.cloned.1.call-start = ((), (), s32[]{:S(2)}) async-start(), calls=%async_computation.15 | async-start | bytes 7077888 | tf_op jit(solution)/shard_map/all_gather | solution.py:272
  20.7 286.6 %all-gather.21.cloned.1.call-start = ((), (), s32[]{:S(2)}) async-start(), calls=%async_computation.8 | async-start | bytes 5242880 | tf_op jit(solution)/shard_map/all_gather | solution.py:275
  23.3 393.1 %reduce-scatter.8.cloned.1.call-start = ((), (), s32[]{:S(2)}) async-start(), calls=%async_computation.10 | async-start | bytes 7077888 | tf_op jit(solution)/shard_map/reduce_scatter | solution.py:413
  41.0 164.4 %copy-start.2 = (f32[8,192,128]{2,1,0:T(8,128)}, f32[8,192,128]{2,1,0:T(8,128)S(1)}, u32[]{:S(2)}) copy-start(f32[8,192,128]{2,1,0:T(8,128)S(1)} %get-tuple-element.127.sin_ref) | copy-start | bytes 2359300
  222.5 1.0 copy-start.3
  223.4 0.9 copy-start.5
  224.3 0.9 copy-start.7
  253.6 5.1 copy-start.4
  253.6 5.1 copy-start.6
  253.6 5.1 copy-start.8
  258.7 25.4 %copy-start.13 = (bf16[2048,768]{1,0:T(8,128)(2,1)S(1)}, bf16[2048,768]{1,0:T(8,128)(2,1)}, u32[]{:S(2)}) copy-start(bf16[2048,768]{1,0:T(8,128)(2,1)} %all-gather.17.cloned.1.call-done.w_ref) | copy-start | bytes 9437188
  307.3 10.2 copy-start.12
  317.4 16.5 %copy-start.29 = (f32[1536,1024]{1,0:T(8,128)}, f32[1536,1024]{1,0:T(8,128)S(1)}, u32[]{:S(2)}) copy-start(f32[1536,1024]{1,0:T(8,128)S(1)} %fusion.41) | copy-start | bytes 18874372
  317.5 16.5 %copy-start.26 = (bf16[2048,1024]{1,0:T(8,128)(2,1)S(1)}, bf16[2048,1024]{1,0:T(8,128)(2,1)}, u32[]{:S(2)}) copy-start(bf16[2048,1024]{1,0:T(8,128)(2,1)} %all-gather.21.cloned.1.call-done) | copy-start | bytes 12582916
  346.4 115.3 %reduce-scatter.10.cloned.1.call-start = ((), (), s32[]{:S(2)}) async-start(), calls=%async_computation.12 | async-start | bytes 3932160 | tf_op jit(solution)/shard_map/reduce_scatter | solution.py:402
  355.7 161.7 %reduce-scatter.14.cloned.1.call-start = ((), (), s32[]{:S(2)}) async-start(), calls=%async_computation.14 | async-start | bytes 5242880 | tf_op jit(solution)/shard_map/reduce_scatter | solution.py:394
  367.1 215.6 %reduce-scatter.12.cloned.1.call-start = ((), (), s32[]{:S(2)}) async-start(), calls=%async_computation.13 | async-start | bytes 6553600 | tf_op jit(solution)/shard_map/reduce_scatter | solution.py:382
  386.5 11.3 %copy-start.11 = (bf16[4,64,2048]{2,1,0:T(8,128)(2,1)S(1)}, bf16[4,64,2048]{2,1,0:T(8,128)(2,1)}, u32[]{:S(2)}) copy-start(bf16[4,64,2048]{2,1,0:T(8,128)(2,1)} %slice.109) | copy-start | bytes 3145732
  386.6 268.8 %reduce-scatter.6.cloned.1.call-start = ((), (), s32[]{:S(2)}) async-start(), calls=%async_computation.9 | async-start | bytes 7077888 | tf_op jit(solution)/shard_map/reduce_scatter | solution.py:410
  402.5 1.1 copy-start.9
  402.5 2.0 copy-start.10
  402.5 377.7 %all-reduce.3.cloned.1.call-start = ((), (), s32[]{:S(2)}) async-start(), calls=%async_computation.11 | async-start | bytes 163840 | tf_op jit(solution)/shard_map/psum | solution.py:442
  421.6 0.6 copy-start.15
  422.3 426.3 %all-gather.25.cloned.1.call-start = ((), (), s32[]{:S(2)}) async-start(), calls=%async_computation.16 | async-start | bytes 7077888 | tf_op jit(solution)/shard_map/all_gather | solution.py:272
  461.7 469.3 %all-gather.29.cloned.1.call-start = ((), (), s32[]{:S(2)}) async-start(), calls=%async_computation.18 | async-start | bytes 9437184 | tf_op jit(solution)/shard_map/all_gather | solution.py:272
  517.4 513.2 %all-gather.27.cloned.1.call-start = ((), (), s32[]{:S(2)}) async-start(), calls=%async_computation.17 | async-start | bytes 11796480 | tf_op jit(solution)/shard_map/all_gather | solution.py:272
  783.9 271.3 %copy-start.16 = (f32[512]{0:T(512)}, f32[512]{0:T(512)S(1)}, u32[]{:S(2)}) copy-start(f32[512]{0:T(512)S(1)} %dynamic_slice.168) | copy-start | bytes 6148
  1043.4 12.4 %copy-start.1 = (bf16[512,2048]{1,0:T(8,128)(2,1)S(1)}, bf16[512,2048]{1,0:T(8,128)(2,1)}, u32[]{:S(2)}) copy-start(bf16[512,2048]{1,0:T(8,128)(2,1)} %param.26) | copy-start | bytes 6291460
Sparse Core Ops, SparseCore 0:
  10.4 64.7 all-gather.18
  77.7 43.9 all-gather.16
  123.3 64.7 all-gather.14
  190.2 63.3 all-gather.22
  255.9 51.3 all-gather.20
  346.5 69.8 reduce-scatter.7
  419.4 42.3 reduce-scatter.9
  464.7 52.6 reduce-scatter.13
  521.2 61.4 reduce-scatter.11
  585.5 69.8 reduce-scatter.5
  662.5 117.7 all-reduce.2
  781.9 66.6 all-gather.24
  850.3 80.6 all-gather.28
  932.6 97.9 all-gather.26
